TPU v7x, 256 devices: a whole 4x4x8 slice. The times are simulated.
256 devices in a mesh: seq: 32 (over z_lo, x, core), uly: 8 (over y, z_hi).
Axes of the slice: x: 4, y: 4, z: 8 (z_hi: 2, z_lo: 4; z = z_hi * 4 + z_lo), core: 2. Of those that a mesh axis runs over, the one named last changes fastest.
Arguments:
- tokens: bfloat16 [16384, 3072], P(('seq', 'uly')), may hold values from -6 to 6
- mod_shift: float32 [3072], replicated, may hold values from -3 to 3
- mod_scale: float32 [3072], replicated, may hold values from -0.5 to 0.5
- mod_gate: float32 [3072], replicated, may hold values from 0.5 to 2
- w_query: bfloat16 [3072, 2048], P(None, 'uly'), may hold values from -0.109375 to 0.109375
- w_key: bfloat16 [3072, 2048], P(None, 'uly'), may hold values from -0.109375 to 0.109375
- w_value: bfloat16 [3072, 2048], P(None, 'uly'), may hold values from -0.109375 to 0.109375
- q_gain: float32 [128], replicated, may hold values from 0.5 to 10
- k_gain: float32 [128], replicated, may hold values from 0.5 to 10
- w_out: bfloat16 [2048, 3072], P('uly'), may hold values from -0.125 to 0.125
- kv_blocks: int32 [128, 50], P('seq'), may hold values from 0 to 127, as said below
- kv_count: int32 [128], P('seq'), may hold values from 8 to 50
Outputs:
- branch_out: bfloat16 [16384, 3072], P(('seq', 'uly'))
Inputs may be any that keep to these rules, and one draw needn't show every extreme that they name: `kv_blocks`: each row names distinct key blocks. The attended set of a query block always holds every block of its own frame and of the frames beside it. From any one frame at distance two or more, the attended sets of all query blocks of one frame together hold at most 2 blocks; entries past kv_count are other blocks and are ignored.
All inputs are finite; a program needn't handle non-finite values.
Results may differ from a plain program's by a relative error of at most 0.025.
The roundings to bfloat16 on the way count: a program that leaves them out, or rounds other values in their place, can miss the bound.
Values may be sent and summed in bfloat16 or wider, within the bound.
A program may use at most 192 MiB of HBM per device.

v0:
```python
import jax
import jax.numpy as jnp
from jax import lax
from jax.sharding import PartitionSpec as P

BLK = 128


eps = 1e-06


def modulate(tokens, mod_shift, mod_scale):
    values = tokens.astype(jnp.float32)
    center = jnp.mean(values, axis=-1, keepdims=True)
    spread = jnp.mean(jnp.square(values - center), axis=-1, keepdims=True)
    normed = (values - center) * lax.rsqrt(spread + eps)
    return (normed * (1.0 + mod_scale) + mod_shift).astype(jnp.bfloat16)


def head_norm(projected, gain, heads):
    shaped = projected.reshape(projected.shape[0], heads, gain.shape[0])
    power = jnp.mean(jnp.square(shaped), axis=-1, keepdims=True)
    return (shaped * lax.rsqrt(power + eps) * gain).astype(jnp.bfloat16)


def body(
    tokens,
    mod_shift,
    mod_scale,
    mod_gate,
    w_query,
    w_key,
    w_value,
    q_gain,
    k_gain,
    w_out,
    kv_blocks,
    kv_count,
):
    head_dim = q_gain.shape[0]
    width = w_query.shape[1]
    heads_here = width // head_dim
    listed_max = kv_blocks.shape[1]
    scale = head_dim ** (-0.5)
    modded = modulate(tokens, mod_shift, mod_scale)
    joined = jnp.concatenate([w_query, w_key, w_value], axis=1)
    projected = jnp.dot(
        lax.all_gather(modded, "uly", axis=0, tiled=True),
        joined,
        preferred_element_type=jnp.float32,
    )
    queries = head_norm(projected[:, :width], q_gain, heads_here)
    keys = head_norm(projected[:, width : 2 * width], k_gain, heads_here)
    values = projected[:, 2 * width :].astype(jnp.bfloat16)
    frame_rows = queries.shape[0]
    paired = jnp.stack([keys.reshape(frame_rows, width), values], axis=1)
    valid = jnp.arange(listed_max, dtype=jnp.int32)[None, :] < kv_count[:, None]
    piece = lax.all_gather(paired, "seq", axis=0, tiled=True)
    peak_old = jnp.full((heads_here, frame_rows), -1e30, jnp.float32)
    count = piece.shape[0]
    piece_blocks = jnp.arange(count, dtype=jnp.int32) // BLK
    member = jnp.any(
        (kv_blocks[:, :, None] == piece_blocks[None, None, :]) & valid[:, :, None], axis=1
    )
    piece_keys = piece[:, 0].reshape(count, heads_here, head_dim)
    piece_values = piece[:, 1].reshape(count, heads_here, head_dim)
    scores = (
        jnp.einsum("qhd,khd->hqk", queries, piece_keys, preferred_element_type=jnp.float32) * scale
    )
    mask = jnp.repeat(member, BLK, axis=0)[None, :, :]
    scores = jnp.where(mask, scores, -1e30)
    peak = jnp.maximum(peak_old, jnp.max(scores, axis=-1))
    weights = jnp.where(mask, jnp.exp(scores - peak[:, :, None]), 0.0)
    total = jnp.sum(weights, axis=-1)
    summed = jnp.einsum(
        "hqk,khd->hqd",
        weights.astype(jnp.bfloat16),
        piece_values,
        preferred_element_type=jnp.float32,
    )
    peak, total, summed = (peak, total, summed)
    attended = (
        jnp.transpose(summed / total[:, :, None], (1, 0, 2))
        .astype(jnp.bfloat16)
        .reshape(frame_rows, width)
    )
    summed_out = lax.psum_scatter(
        jnp.dot(attended, w_out, preferred_element_type=jnp.float32).astype(jnp.bfloat16),
        "uly",
        scatter_dimension=0,
        tiled=True,
    ).astype(jnp.float32)
    return (summed_out * mod_gate).astype(jnp.bfloat16)


def solution(mesh):
    placed = (
        P(("seq", "uly"), None),
        P(),
        P(),
        P(),
        P(None, "uly"),
        P(None, "uly"),
        P(None, "uly"),
        P(),
        P(),
        P("uly", None),
        P("seq", None),
        P("seq"),
    )
    return jax.shard_map(
        body, mesh=mesh, in_specs=placed, out_specs=P(("seq", "uly"), None), check_vma=False
    )
```

profile of v0, /device:TPU:8, one launch (start us, length us, event | category | flops | bytes accessed | tf_op | source)
XLA Modules:
  0.0 467.5 jit_solution(3995127188476081172)
XLA Ops:
  6.5 1.3 convert_reduce_fusion
  7.8 1.3 fusion.25
  9.1 0.7 broadcast_add_fusion
  9.8 1.9 fusion.28
  11.8 0.0 all-gather.5.cloned.1.call-start
  11.8 0.7 broadcast_bitcast_fusion
  12.5 93.5 %all-gather.3.cloned.1.call-done = bf16[512,3072]{1,0:T(8,128)(2,1)} async-done(((bf16[64,3072]{1,0:T(8,128)(2,1)}), bf16[512,3072]{1,0:T(8,128)(2,1)}) %all-gather.3.cloned.1.call-update) | async-done | bytes 3145744 | tf_op jit(solution)/shard_map/all_gather | solution.py:48
  106.1 5.9 %fusion.8 = f32[512,768]{1,0:T(8,128)S(1)} fusion(bf16[512,3072]{1,0:T(8,128)(2,1)} %all-gather.3.cloned.1.call-done, bf16[3072,256]{1,0:T(8,128)(2,1)} %param.18, bf16[3072,256]{1,0:T(8,128)(2,1)} %param.17, bf16[3072,256]{1,0:T(8,128)(2,1)} %param.16), kind=kOutput, calls=%fused_computation.10 | convolution fusion | flops 2430074880 | bytes 9437184 | tf_op jit(solution)/shard_map/dot_general | solution.py:47
  112.0 0.8 slice_multiply_fusion
  112.8 2.1 square.15
  114.9 2.4 reduce_sum.48
  117.3 1.0 add_rsqrt_fusion
  118.3 0.6 mul.80
  118.9 0.9 fusion.42
  119.8 0.9 pad_maximum_fusion
  120.7 0.0 reduce-scatter.2.cloned.1.call-start
  120.7 0.1 copy.24
  120.9 5.4 %and_reduce_fusion = pred[4,16384]{1,0:T(4,128)(4,1)S(1)} fusion(s32[16384]{0:T(1024)S(1)} %add_select_fusion, s32[4,50]{0,1:T(8,128)S(1)} %copy.24, pred[4,50]{0,1:T(8,128)(4,1)S(1)} %iota_compare_fusion), kind=kLoop, calls=%fused_computation.7 | loop fusion | flops 9764864 | bytes 132072 | tf_op jit(solution)/shard_map/reduce_or | solution.py:62
  126.3 1.3 reshape.90
  127.6 0.6 multiply_reduce_fusion
  128.3 0.9 multiply_convert_fusion.1
  129.2 87.2 %all-gather.5.cloned.1.call-done = bf16[16384,2,256]{2,0,1:T(8,128)(2,1)} async-done(((bf16[512,2,256]{2,0,1:T(8,128)(2,1)}), bf16[16384,2,256]{2,0,1:T(8,128)(2,1)}) %all-gather.5.cloned.1.call-update) | async-done | bytes 16777232 | tf_op jit(solution)/shard_map/all_gather | solution.py:58
  216.4 11.3 %fusion.41 = (bf16[16384,1,256]{2,0,1:T(8,128)(2,1)}, bf16[16384,1,256]{2,0,1:T(8,128)(2,1)}) fusion(bf16[16384,2,256]{2,0,1:T(8,128)(2,1)} %all-gather.5.cloned.1.call-done), kind=kLoop, calls=%fused_computation.59 | loop fusion | bytes 33554432 | tf_op jit(solution)/shard_map/slice | solution.py:65
  227.8 12.5 %reshape_squeeze.6 = bf16[16384,2,128]{2,1,0:T(2,128)(2,1)} reshape(bf16[16384,1,256]{2,0,1:T(8,128)(2,1)} %get-tuple-element.5) | data formatting | bytes 16777216 | tf_op jit(solution)/shard_map/reshape;squeeze | solution.py:65
  240.3 12.0 %copy.32 = bf16[16384,1,256]{0,2,1:T(8,128)(2,1)} copy(bf16[16384,1,256]{2,0,1:T(8,128)(2,1)} %get-tuple-element.6) | data formatting | bytes 16777216 | tf_op jit(solution)/shard_map/reshape;squeeze | solution.py:66
  252.2 6.7 %broadcast_in_dim.24 = pred[4,128,16384]{2,1,0:T(8,128)(4,1)} broadcast(pred[4,16384]{1,0:T(4,128)(4,1)S(1)} %and_reduce_fusion), dimensions={0,2} | broadcast | bytes 8454144 | tf_op jit(solution)/shard_map/broadcast_in_dim | solution.py:70
  259.0 31.2 %fusion = (f32[2,512]{1,0:T(2,128)S(1)}, f32[2,512,16384]{2,1,0:T(8,128)}) fusion(pred[512,16384]{1,0:T(8,128)(4,1)} %bitcast.31, bf16[16384,2,128]{2,1,0:T(2,128)(2,1)} %reshape_squeeze.6, bf16[512,2,128]{2,1,0:T(2,128)(2,1)S(1)} %multiply_convert_fusion.1), kind=kOutput, calls=%fused_computation.2 | convolution fusion | flops 4345297920 | bytes 84152320 | tf_op jit(solution)/shard_map/qhd,khd->hqk/dot_general | solution.py:68
  290.2 24.2 %fusion.1 = f32[2,512]{1,0:T(2,128)S(1)} fusion(f32[2,512,16384]{2,1,0:T(8,128)} %get-tuple-element.10, f32[2,512]{1,0:T(2,128)S(1)} %broadcast_maximum_fusion, pred[512,16384]{1,0:T(8,128)(4,1)} %bitcast.32), kind=kLoop, calls=%fused_computation.3 | loop fusion | flops 83885056 | bytes 75505664 | tf_op jit(solution)/shard_map/reduce_sum | solution.py:74
  314.4 30.4 %fusion.20 = bf16[512,2,128]{0,2,1:T(8,128)(2,1)S(1)} fusion(bf16[16384,2,128]{0,2,1:T(8,128)(2,1)} %bitcast.34, f32[2,512,16384]{2,1,0:T(8,128)} %get-tuple-element.10, f32[2,512]{1,0:T(2,128)S(1)} %broadcast_maximum_fusion, pred[512,16384]{1,0:T(8,128)(4,1)} %bitcast.33, f32[512,2]{0,1:T(2,128)S(1)} %bitcast.37), kind=kOutput, calls=%fused_computation.19 | convolution fusion | flops 4379115520 | bytes 84156416 | tf_op jit(solution)/shard_map/hqk,khd->hqd/dot_general | solution.py:75
  344.8 2.7 convolution_convert_fusion
  347.5 111.6 %reduce-scatter.2.cloned.1.call-done = bf16[64,3072]{1,0:T(8,128)(2,1)} async-done(((bf16[512,3072]{1,0:T(8,128)(2,1)}), bf16[64,3072]{1,0:T(8,128)(2,1)}) %reduce-scatter.2.cloned.1.call-update) | async-done | bytes 393232 | tf_op jit(solution)/shard_map/reduce_scatter | solution.py:87
  459.2 1.8 multiply_convert_fusion
  (21 shorter events, 0.2 us)
Async XLA Ops:
  6.5 338.3 %copy-start = (bf16[256,3072]{1,0:T(8,128)(2,1)S(1)}, bf16[256,3072]{1,0:T(8,128)(2,1)}, u32[]{:S(2)}) copy-start(bf16[256,3072]{1,0:T(8,128)(2,1)} %param.21) | copy-start | bytes 4718596
  6.5 99.5 %all-gather.3.cloned.1.call-start = ((), (), s32[]{:S(2)}) async-start(), calls=%async_computation.1 | async-start | bytes 3538944 | tf_op jit(solution)/shard_map/all_gather | solution.py:48
  11.8 204.6 %all-gather.5.cloned.1.call-start = ((), (), s32[]{:S(2)}) async-start(), calls=%async_computation.2 | async-start | bytes 17301504 | tf_op jit(solution)/shard_map/all_gather | solution.py:58
  111.9 8.8 %copy-start.2 = (s32[4,50]{1,0:T(4,128)S(1)}, s32[4,50]{1,0:T(4,128)}, u32[]{:S(2)}) copy-start(s32[4,50]{1,0:T(4,128)} %param.22) | copy-start | bytes 2404
  112.0 8.9 %copy-start.4 = (s32[4]{0:T(128)S(1)}, s32[4]{0:T(128)}, u32[]{:S(2)}) copy-start(s32[4]{0:T(128)} %param.23) | copy-start | bytes 52
  112.0 16.3 %copy-start.3 = (f32[128]{0:T(128)S(1)}, f32[128]{0:T(128)}, u32[]{:S(2)}) copy-start(f32[128]{0:T(128)} %param.19) | copy-start | bytes 1540
  120.7 338.5 %reduce-scatter.2.cloned.1.call-start = ((), (), s32[]{:S(2)}) async-start(), calls=%async_computation.3 | async-start | bytes 3538944 | tf_op jit(solution)/shard_map/reduce_scatter | solution.py:87
  344.8 114.4 %copy-start.1 = (f32[3072]{0:T(1024)S(1)}, f32[3072]{0:T(1024)}, u32[]{:S(2)}) copy-start(f32[3072]{0:T(1024)} %param.15) | copy-start | bytes 36868
Sparse Core Ops, SparseCore 0:
  11.9 94.0 all-gather.2
  120.8 95.5 all-gather.4
  347.7 111.4 reduce-scatter.1
where the time goes:
time: 469 us; the launch traced here: 468 us
  waiting for transfers between devices  292 us (62%)
  matrix products  70.1 us (15%)
  local copies, waits for them, and re-layouts  47.3 us (10%)
  other arithmetic  44.2 us (9%)
  between operations  13.3 us (3%)
    reduce_scatter x1, waiting for transfers between devices, body(): lax.psum_scatter(jnp.dot(attended, w_out, preferred_element_type=jnp.floa...  112 us
    all_gather x1, waiting for transfers between devices, body(): lax.all_gather(modded, 'uly', axis=0, tiled=True)  93.5 us
    all_gather x1, waiting for transfers between devices, body(): piece = lax.all_gather(paired, 'seq', axis=0, tiled=True)  87.2 us
    dot_general x1, matrix products, body(): jnp.einsum('qhd,khd->hqk', queries, piece_keys, preferred_element_type=jn...  31.2 us
    dot_general x1, matrix products, body(): jnp.einsum('hqk,khd->hqd', weights.astype(jnp.bfloat16), piece_values, pr...  30.4 us
    reduce_sum x1, other arithmetic, body(): total = jnp.sum(weights, axis=-1)  24.2 us
    another operation x1, local copies, waits for them, and re-layouts, body(): piece_keys = piece[:, 0].reshape(count, heads_here, head_dim)  12.5 us
    another operation x1, local copies, waits for them, and re-layouts, body(): piece_values = piece[:, 1].reshape(count, heads_here, head_dim)  12 us
  transfers between devices with their start and end apart: 3, of which 3 were waited for; matrix products, arithmetic and copies ran while one was open for 2% of the time, Pallas kernels for 0%

commit v1 on v0

v1 whole, which is shorter than its diff:
```python
import functools
import math

import jax
import jax.numpy as jnp
from jax import lax
from jax.experimental import pallas as pl
from jax.experimental.pallas import tpu as pltpu
from jax.sharding import PartitionSpec as P

MESH = pl.DeviceIdType.MESH
EPS = 1e-06
D = 3072
HD = 128
LOW = -1e30
CC = D // 2


def pick(cond, a, b):
    return jnp.where(cond, a, b)


def kernel(
    tokens_ref, shift_ref, scale_ref, gate_ref, wq_ref, wk_ref, wv_ref, qg_ref, kg_ref, wo_ref, lists_ref,
    out_ref,
    w, wo, tok, lst, tabv, tabs, stage, qbuf, kv, kvp, m, l, o, attb, atts, part, rfwd, ra, rb, rz, zsend,
    wsem, lsem, tsend, trecv, ssend, srecv, ksend, krecv, asend, arecv, rsend, rrecv,
):
    s = lax.axis_index("seq")
    u = lax.axis_index("uly")
    zl, x, c = s // 8, (s // 2) % 4, s % 2
    i, p = zl % 2, zl // 2
    y, zh = u // 2, u % 2
    d = 1 - 2 * c

    def xdev(e):
        return (zl * 8 + ((x + e + 8) % 4) * 2 + c, u)

    def yy(e):
        return (y + e + 8) % 4

    def ydev(e):
        return (s, yy(e) * 2 + zh)

    core_dev = (s + 1 - 2 * c, u)
    pair_dev = (s + 8 * (1 - 2 * i), u)
    far_dev = (s + 16 * (1 - 2 * p), u)
    anti_dev = (s, y * 2 + 1 - zh)

    def rcopy(src, dst, ss, rs, dev):
        return pltpu.make_async_remote_copy(
            src_ref=src, dst_ref=dst, send_sem=ss, recv_sem=rs, device_id=dev, device_id_type=MESH
        )

    wcopies = [pltpu.make_async_copy(r, w.at[n], wsem.at[n]) for n, r in enumerate((wq_ref, wk_ref, wv_ref))]
    wcopies.append(pltpu.make_async_copy(wo_ref, wo, wsem.at[3]))
    for cp in wcopies:
        cp.start()

    barrier = pltpu.get_barrier_semaphore()
    for dev in (core_dev, pair_dev, far_dev, anti_dev, xdev(1), xdev(-1), ydev(1), ydev(-1)):
        pl.semaphore_signal(barrier, inc=1, device_id=dev, device_id_type=MESH)

    vals = tokens_ref[...].astype(jnp.float32)
    center = jnp.mean(vals, axis=-1, keepdims=True)
    vals = vals - center
    spread = jnp.mean(vals * vals, axis=-1, keepdims=True)
    vals = vals * lax.rsqrt(spread + EPS)
    tok[0, y] = (vals * (1.0 + scale_ref[...]) + shift_ref[...]).astype(jnp.bfloat16)
    lst[i] = lists_ref[...]

    pl.semaphore_wait(barrier, 8)

    def half_rows(n):
        return pl.ds(32 * n, 32)

    def t_anti(n):
        return rcopy(tok.at[0, y, half_rows(n)], tok.at[1, y, half_rows(n)], tsend.at[n], trecv.at[n], anti_dev)

    def t_own(e):
        k = 2 if e == 1 else 3
        return rcopy(tok.at[0, y], tok.at[0, y], tsend.at[k], trecv.at[k], ydev(d * e))

    def t_own_in(e):
        k = 2 if e == 1 else 3
        sl = yy(-d * e)
        return rcopy(tok.at[0, sl], tok.at[0, sl], tsend.at[k], trecv.at[k], ydev(d * e))

    def t_fwd():
        sl = yy(-d)
        return rcopy(tok.at[0, sl], tok.at[0, sl], tsend.at[4], trecv.at[4], ydev(d))

    def t_fwd_in():
        sl = yy(2)
        return rcopy(tok.at[0, sl], tok.at[0, sl], tsend.at[4], trecv.at[4], ydev(d))

    def t_other(n, e, sl):
        k = 5 + 2 * n + (0 if e == 1 else 1)
        return rcopy(tok.at[1, sl, half_rows(n)], tok.at[1, sl, half_rows(n)], tsend.at[k], trecv.at[k], ydev(d * e))

    def t_other_fwd(n, sl):
        k = 9 + n
        return rcopy(tok.at[1, sl, half_rows(n)], tok.at[1, sl, half_rows(n)], tsend.at[k], trecv.at[k], ydev(d))

    def l_copy(row):
        return rcopy(lst.at[row], lst.at[row], lsem.at[0], lsem.at[1], pair_dev)

    l_copy(i).start()
    t_anti(0).start()
    t_own(1).start()
    t_own(-1).start()
    t_anti(1).start()

    m[...] = jnp.full(m.shape, LOW, jnp.float32)
    l[...] = jnp.zeros(l.shape, jnp.float32)
    o[...] = jnp.zeros(o.shape, jnp.float32)
    l_copy(1 - i).wait_recv()
    first, second = lst[0], lst[1]
    listed = jnp.concatenate([first[0:4], second[0:4]], axis=0)
    counts = jnp.concatenate([first[4:8], second[4:8]], axis=0)
    lane = lax.broadcasted_iota(jnp.int32, (8, 128), 1)
    row = lax.broadcasted_iota(jnp.int32, (8, 128), 0)
    listed = jnp.where(lane < counts, listed, -1)
    member = jnp.zeros((8, 128), jnp.int32)
    for e in range(50):
        member = jnp.where(listed[:, e : e + 1] == lane, 1, member)
    union = jnp.where(
        row < 4,
        jnp.max(member[0:4], axis=0, keepdims=True),
        jnp.max(member[4:8], axis=0, keepdims=True),
    )

    def ahead(a, n):
        return a if n == 0 else pltpu.roll(a, 128 - n, 1)

    us = [ahead(union, n) > 0 for n in range(4)]
    ms = [ahead(member, n) for n in range(4)]
    f0 = 2 * p * 8 + x * 2 + c
    near = jnp.abs((lane >> 2) - jnp.where(row < 4, f0, f0 + 8)) <= 1
    idx0 = jnp.where(us[0], 0, jnp.where(us[1], 1, jnp.where(us[2], 2, 3)))
    idx1 = jnp.where(us[3], 3, jnp.where(us[2], 2, jnp.where(us[1], 1, 0)))
    idx1 = jnp.where(idx1 == idx0, (idx0 + 1) & 3, idx1)
    idx0 = jnp.where(near, 0, idx0)
    idx1 = jnp.where(near, 1, idx1)

    def at(idx):
        return jnp.where(idx == 0, ms[0], jnp.where(idx == 1, ms[1], jnp.where(idx == 2, ms[2], ms[3])))

    tabv[0] = idx0
    tabv[1] = idx1
    tabv[2] = at(idx0)
    tabv[3] = at(idx1)
    tcopy = pltpu.make_async_copy(tabv, tabs, wsem.at[4])
    tcopy.start()
    tcopy.wait()
    l_copy(i).wait_send()

    for cp in wcopies[:3]:
        cp.wait()

    slot_own = p * 8 + x * 2 + c

    def project(h):
        a = tok[h].reshape(256, D)
        for n, gain in enumerate((qg_ref, kg_ref, None)):
            acc = jnp.dot(a, w[n], preferred_element_type=jnp.float32)
            for hd in range(2):
                piece = acc[:, hd * HD : (hd + 1) * HD]
                if gain is not None:
                    power = jnp.mean(piece * piece, axis=-1, keepdims=True)
                    piece = piece * lax.rsqrt(power + EPS) * gain[...]
                stage[h, hd, n] = piece.astype(jnp.bfloat16)

    def s_kv(h, who):
        return rcopy(stage.at[h, 1 - i, pl.ds(1, 2)], kv.at[slot_own, h, who], ssend.at[h, 0], srecv.at[h, 0], pair_dev)

    def s_q(h, who):
        return rcopy(stage.at[h, 1 - i, 0], qbuf.at[who, h], ssend.at[h, 1], srecv.at[h, 1], pair_dev)

    def swap_out(h):
        s_kv(h, i).start()
        s_q(h, i).start()
        kv[slot_own, h, i] = stage[h, i, 1:3]
        qbuf[i, h] = stage[h, i, 0]

    def k_copy(h, slot, e, dev):
        return rcopy(kv.at[slot, h], kv.at[slot, h], ksend.at[h, e], krecv.at[h, slot], dev)

    def swap_in(h):
        s_kv(h, 1 - i).wait_recv()
        k_copy(h, slot_own, 0, far_dev).start()
        k_copy(h, slot_own, 1, xdev(1)).start()
        k_copy(h, slot_own, 2, xdev(-1)).start()
        k_copy(h, slot_own, 3, core_dev).start()
        s_q(h, 1 - i).wait_recv()

    t_own_in(1).wait_recv()
    t_fwd().start()
    t_anti(0).wait_recv()
    t_other(0, 1, y).start()
    t_other(0, -1, y).start()
    t_own_in(-1).wait_recv()
    t_fwd_in().wait_recv()
    project(0)
    swap_out(0)
    t_anti(1).wait_recv()
    t_other(1, 1, y).start()
    t_other(1, -1, y).start()
    t_other(0, 1, yy(-d)).wait_recv()
    t_other_fwd(0, yy(-d)).start()
    swap_in(0)

    factor = (HD ** -0.5) * math.log2(math.e)
    lane1 = lax.broadcasted_iota(jnp.int32, (1, 128), 1)

    def attend(fi, h, parts):
        q = qbuf[fi, h]
        old = m[fi, h]
        new = old
        tiles = []
        for keys, _, bias in parts:
            scores = lax.dot_general(q, keys, (((1,), (1,)), ((), ())), preferred_element_type=jnp.float32) * factor
            if bias is not None:
                scores = (scores.reshape(4, 64, 256) + bias).reshape(256, 256)
            tiles.append(scores)
            new = jnp.maximum(new, jnp.max(scores, axis=1, keepdims=True))
        decay = jnp.exp2(old - new)
        total = l[fi, h] * decay
        summed = o[fi, h] * decay
        for scores, (_, values, _) in zip(tiles, parts):
            left = jnp.exp2(scores[:, :128] - new)
            right = jnp.exp2(scores[:, 128:] - new)
            total = total + (left + right)
            weights = jnp.concatenate([left.astype(jnp.bfloat16), right.astype(jnp.bfloat16)], axis=1)
            summed = summed + jnp.dot(weights, values, preferred_element_type=jnp.float32)
        m[fi, h] = new
        l[fi, h] = total
        o[fi, h] = summed

    def near_pass(n, carry):
        fi, df = n // 3, n % 3 - 1
        f = (2 * p + fi) * 8 + x * 2 + c + df

        @pl.when(jnp.logical_and(f >= 0, f <= 31))
        def _():
            fz = f // 8
            slot = (fz // 2) * 8 + f % 8
            keys = jnp.concatenate([kv[slot, h, fz % 2, 0, 128:256] for h in range(2)], axis=0)
            values = jnp.concatenate([kv[slot, h, fz % 2, 1, 128:256] for h in range(2)], axis=0)
            for h in range(2):
                attend(fi, h, [(keys, values, None)])

        return carry

    def chosen(fi, base):
        rows, bias = [], []
        for ff in range(2):
            at4 = (base + 8 * ff) * 4
            rows.append([tabs[t, fi * 4, at4] for t in range(2)])
            rowsb = []
            for b in range(4):
                b0 = jnp.where(tabs[2, fi * 4 + b, at4] > 0, 0.0, LOW)
                b1 = jnp.where(tabs[3, fi * 4 + b, at4] > 0, 0.0, LOW)
                rowsb.append(jnp.where(lane1 < 64, b0, b1).reshape(1, 1, 128))
            bias.append(jnp.concatenate(rowsb, axis=0))
        bias = jnp.concatenate(bias, axis=2)

        def group(kh):
            return tuple(
                jnp.concatenate([kvp[kh, ff, t, rows[ff][e]] for ff in range(2) for e in range(2)], axis=0)
                for t in range(2)
            ) + (bias,)

        return group

    def step(h, k, carry):
        j, oc = k // 2, k % 2

        if h == 0:

            @pl.when(k == 2)
            def _():
                t_other(1, 1, yy(-d)).wait_recv()
                t_other_fwd(1, yy(-d)).start()

            @pl.when(k == 4)
            def _():
                for e in range(2):
                    t_other(e, -1, yy(d)).wait_recv()
                    t_other_fwd(e, yy(2)).wait_recv()
                project(1)
                swap_out(1)

            @pl.when(k == 8)
            def _():
                swap_in(1)

        else:

            @pl.when(k == 14)
            def _():
                lax.fori_loop(0, 6, near_pass, 0)

        dp = pick(j == 3, 1, pick(j >= 5, 1, 0))
        dxs = pick(j % 4 == 1, -1, pick(j == 2, 1, pick(j == 6, 1, pick(j == 4, 2, pick(j == 7, 2, 0)))))
        dd = d * (1 - 2 * oc)
        slot = ((p + dp) % 2) * 8 + ((x + dd * dxs + 8) % 4) * 2 + (c + oc) % 2

        @pl.when(k > 0)
        def _():
            k_copy(h, slot, 0, core_dev).wait_recv()

        @pl.when(jnp.logical_and(oc == 0, j > 0))
        def _():
            k_copy(h, slot, 3 + j, core_dev).start()

        @pl.when(jnp.logical_and(oc == 0, j % 4 == 1))
        def _():
            k_copy(h, slot, 11 + j // 4, xdev(d)).start()

        @pl.when(jnp.logical_and(oc == 0, j == 3))
        def _():
            k_copy(h, slot, 13, xdev(1)).start()
            k_copy(h, slot, 14, xdev(-1)).start()

        for kh in range(h + 1):
            kvp[kh] = kv[slot, kh].reshape(2, 2, 4, 64, HD)
        base = (slot // 8) * 16 + slot % 8
        for fi in range(2):
            group = chosen(fi, base)
            late = group(h)
            attend(fi, 0, [late])
            if h == 1:
                attend(fi, 1, [group(0), late])
        return carry

    lax.fori_loop(0, 16, functools.partial(step, 0), 0)
    lax.fori_loop(0, 16, functools.partial(step, 1), 0)

    def result(fi, h):
        total = jnp.sum(l[fi, h], axis=1, keepdims=True)
        return (o[fi, h] / total).astype(jnp.bfloat16)

    def a_copy(h, head):
        return rcopy(atts.at[h], attb.at[head, h], asend.at[h], arecv.at[h], pair_dev)

    for h in (1, 0):
        atts[h] = result(1 - i, h)
        a_copy(h, i).start()
    for h in (1, 0):
        attb[i, h] = result(i, h)
    wcopies[3].wait()

    def r_out(q, dest):
        return rcopy(part.at[q, dest], rfwd.at[q], rsend.at[q, 0], rrecv.at[q, 0], ydev(d))

    def r_a(q):
        return rcopy(part.at[q, yy(d)], ra.at[q], rsend.at[q, 1], rrecv.at[q, 1], ydev(d))

    def r_b(q):
        return rcopy(part.at[q, yy(-d)], rb.at[q], rsend.at[q, 2], rrecv.at[q, 2], ydev(-d))

    def r_z(cc):
        return rcopy(zsend.at[cc], rz.at[cc], rsend.at[2 + cc, 3], rrecv.at[2 + cc, 3], anti_dev)

    for h in (1, 0):
        a_copy(h, 1 - i).wait_recv()
        rows = jnp.concatenate([attb[0, h], attb[1, h]], axis=1)
        for cc in range(2):
            q = 2 * h + cc

            def cols(t, carry):
                at_col = pl.multiple_of(cc * CC + t * 256, 256)
                res = jnp.dot(rows, wo[:, pl.ds(at_col, 256)], preferred_element_type=jnp.float32)
                part[q, :, :, pl.ds(pl.multiple_of(t * 256, 256), 256)] = res.astype(jnp.bfloat16).reshape(4, 64, 256)
                return carry

            lax.fori_loop(0, CC // 256, cols, 0)
            r_out(q, yy(2)).start()
            r_b(q).start()

    def chain(q):
        r_out(q, yy(2)).wait_recv()
        part[q, yy(d)] = (part[q, yy(d)].astype(jnp.float32) + rfwd[q].astype(jnp.float32)).astype(jnp.bfloat16)
        r_a(q).start()

    def gathered(q):
        r_a(q).wait_recv()
        r_b(q).wait_recv()
        return part[q, y].astype(jnp.float32) + ra[q].astype(jnp.float32) + rb[q].astype(jnp.float32)

    def to_anti(cc):
        zsend[cc] = gathered(2 + cc).astype(jnp.bfloat16)
        r_z(cc).start()

    def finish(cc):
        total = gathered(cc)
        r_z(cc).wait_recv()
        cols = slice(cc * CC, (cc + 1) * CC)
        out_ref[:, cols] = ((total + rz[cc].astype(jnp.float32)) * gate_ref[:, cols]).astype(jnp.bfloat16)

    chain(2)
    chain(3)
    to_anti(0)
    chain(0)
    to_anti(1)
    chain(1)
    finish(0)
    finish(1)

    for n in range(2):
        t_anti(n).wait_send()
        t_other(n, 1, y).wait_send()
        t_other(n, -1, y).wait_send()
        t_other_fwd(n, yy(-d)).wait_send()
    t_own(1).wait_send()
    t_own(-1).wait_send()
    t_fwd().wait_send()
    for h in range(2):
        s_kv(h, i).wait_send()
        s_q(h, i).wait_send()
        a_copy(h, i).wait_send()
        for e in range(15):
            k_copy(h, slot_own, e, core_dev).wait_send()
    for q in range(4):
        r_out(q, yy(2)).wait_send()
        r_a(q).wait_send()
        r_b(q).wait_send()
    for cc in range(2):
        r_z(cc).wait_send()


def body(tokens, mod_shift, mod_scale, mod_gate, w_query, w_key, w_value, q_gain, k_gain, w_out, kv_blocks, kv_count):
    lists = jnp.concatenate(
        [jnp.pad(kv_blocks, ((0, 0), (0, 78))), jnp.broadcast_to(kv_count[:, None], (4, 128))], axis=0
    )
    vmem = pl.BlockSpec(memory_space=pltpu.VMEM)
    hbm = pl.BlockSpec(memory_space=pl.ANY)
    bf16, f32 = jnp.bfloat16, jnp.float32
    dma = pltpu.SemaphoreType.DMA
    return pl.pallas_call(
        kernel,
        out_shape=jax.ShapeDtypeStruct((64, D), bf16),
        in_specs=[vmem, vmem, vmem, vmem, hbm, hbm, hbm, vmem, vmem, hbm, vmem],
        out_specs=vmem,
        scratch_shapes=[
            pltpu.VMEM((3, D, 256), bf16),
            pltpu.VMEM((256, D), bf16),
            pltpu.VMEM((2, 4, 64, D), bf16),
            pltpu.VMEM((2, 8, 128), jnp.int32),
            pltpu.VMEM((4, 8, 128), jnp.int32),
            pltpu.SMEM((4, 8, 128), jnp.int32),
            pltpu.VMEM((2, 2, 3, 256, HD), bf16),
            pltpu.VMEM((2, 2, 256, HD), bf16),
            pltpu.VMEM((16, 2, 2, 2, 256, HD), bf16),
            pltpu.VMEM((2, 2, 2, 4, 64, HD), bf16),
            pltpu.VMEM((2, 2, 256, 128), f32),
            pltpu.VMEM((2, 2, 256, 128), f32),
            pltpu.VMEM((2, 2, 256, HD), f32),
            pltpu.VMEM((2, 2, 256, HD), bf16),
            pltpu.VMEM((2, 256, HD), bf16),
            pltpu.VMEM((4, 4, 64, CC), bf16),
            pltpu.VMEM((4, 64, CC), bf16),
            pltpu.VMEM((4, 64, CC), bf16),
            pltpu.VMEM((4, 64, CC), bf16),
            pltpu.VMEM((2, 64, CC), bf16),
            pltpu.VMEM((2, 64, CC), bf16),
            dma((5,)),
            dma((2,)),
            dma((11,)),
            dma((11,)),
            dma((2, 2)),
            dma((2, 2)),
            dma((2, 15)),
            dma((2, 16)),
            dma((2,)),
            dma((2,)),
            dma((4, 4)),
            dma((4, 4)),
        ],
        compiler_params=pltpu.CompilerParams(
            collective_id=0, has_side_effects=True, vmem_limit_bytes=48 * 2**20
        ),
        name="radial_block",
    )(
        tokens,
        mod_shift.reshape(1, D),
        mod_scale.reshape(1, D),
        mod_gate.reshape(1, D),
        w_query,
        w_key,
        w_value,
        q_gain.reshape(1, HD),
        k_gain.reshape(1, HD),
        w_out,
        lists,
    )


def solution(mesh):
    placed = (
        P(("seq", "uly"), None),
        P(),
        P(),
        P(),
        P(None, "uly"),
        P(None, "uly"),
        P(None, "uly"),
        P(),
        P(),
        P("uly", None),
        P("seq", None),
        P("seq"),
    )
    return jax.shard_map(
        body, mesh=mesh, in_specs=placed, out_specs=P(("seq", "uly"), None), check_vma=False
    )
```

time: 469 us -> 152 us (0.32)
  waiting for transfers between devices: 292 us -> 0 us
  Pallas kernels: 0 us -> 141 us
  matrix products: 70.1 us -> 0 us
  other arithmetic: 44.2 us -> 0.75 us
  local copies, waits for them, and re-layouts: 47.3 us -> 10.1 us
  between operations: 13.3 us -> 0.02 us
    all_gather x2 -> x0, waiting for transfers between devices: 181 us -> none  [the longest x1 93.5 us: body(): lax.all_gather(modded, 'uly', axis=0, tiled=True)]
    pallas_call x0 -> x1, Pallas kernels: none -> 141 us  [body(): pl.pallas_call(kernel, out_shape=jax.ShapeDtypeStruct((64, D), bf16), in_...]
    reduce_scatter x1 -> x0, waiting for transfers between devices: 112 us -> none  [body(): lax.psum_scatter(jnp.dot(attended, w_out, preferred_element_type=jnp.floa...]
    dot_general x4 -> x0, matrix products: 70.1 us -> none  [the longest x1 31.2 us: body(): jnp.einsum('qhd,khd->hqk', queries, piece_keys, preferred_element_type=jn...]
    reduce_sum x5 -> x0, other arithmetic: 29.8 us -> none  [the longest x1 24.2 us: body(): total = jnp.sum(weights, axis=-1)]
    another operation x3 -> x0, local copies, waits for them, and re-layouts: 24.5 us -> none  [the longest x1 12.5 us: body(): piece_keys = piece[:, 0].reshape(count, heads_here, head_dim)]
    slice x1 -> x0, local copies, waits for them, and re-layouts: 11.3 us -> none  [body(): piece_keys = piece[:, 0].reshape(count, heads_here, head_dim)]
    unnamed x11 -> x19, local copies, waits for them, and re-layouts: 0.14 us -> 9.39 us
  transfers between devices with their start and end apart: 3 -> 0, of which waited for: 3 -> 0; matrix products, arithmetic and copies ran while one was open for 2% -> 0% of each run, Pallas kernels for 0% -> 0%
where the time goes in v1:
time: 152 us
  Pallas kernels  141 us (93%)
  local copies, waits for them, and re-layouts  10.1 us (7%)
    pallas_call x1, Pallas kernels, body(): pl.pallas_call(kernel, out_shape=jax.ShapeDtypeStruct((64, D), bf16), in_...  141 us
    unnamed x19, local copies, waits for them, and re-layouts  9.39 us

profile of v1, /device:TPU:8, one launch (start us, length us, event | category | flops | bytes accessed | tf_op | source)
XLA Modules:
  0.0 151.6 jit_solution(12444800733509770331)
XLA Ops:
  0.0 0.7 pad.6.clone
  0.7 0.8 pad_add_fusion.lists_ref
  1.5 0.0 copy-start
  1.5 1.4 copy-done
  2.9 0.0 copy-start.1
  2.9 1.4 copy-done.1
  4.3 0.0 copy-start.2
  4.3 1.4 copy-done.2
  5.7 0.0 copy-start.3
  5.7 1.0 copy-done.3
  6.7 0.0 copy-start.4
  6.7 0.7 copy-done.4
  7.4 0.0 copy-start.5
  7.4 0.7 copy-done.5
  8.1 0.0 copy-start.6
  8.1 0.7 copy-done.6
  8.8 0.0 copy-start.7
  8.8 0.7 copy-done.7
  9.5 0.0 copy-start.8
  9.5 0.7 copy-done.8
  10.1 140.7 %radial_block.1 = bf16[64,3072]{1,0:T(8,128)(2,1)S(1)} custom-call(bf16[64,3072]{1,0:T(8,128)(2,1)S(1)} %copy-done.3, f32[1,3072]{1,0:T(1,128)S(1)} %bitcast.5, f32[1,3072]{1,0:T(1,128)S(1)} %bitcast.6, f32[1,3072]{1,0:T(1,128)S(1)} %bitcast.7, bf16[3072,256]{1,0:T(8,128)(2,1)S(1)} %copy-done, bf16[3072,256]{1,0:T(8,128)(2,1)S(1)} %copy-done.1, ...), custom_call_target="tpu_custom_call" | custom-call | tf_op jit(solution)/shard_map/radial_block/pallas_call | solution.py:441
  150.8 0.7 copy.14
Async XLA Ops:
  1.5 1.4 copy-start
  2.9 1.4 copy-start.1
  4.3 1.4 copy-start.2
  5.7 1.0 copy-start.3
  6.7 0.7 copy-start.4
  7.4 0.7 copy-start.5
  8.1 0.7 copy-start.6
  8.8 0.7 copy-start.7
  9.5 0.7 copy-start.8

commit v2 on v1

v2 whole, which is shorter than its diff:
```python
import functools
import math

import jax
import jax.numpy as jnp
from jax import lax
from jax.experimental import pallas as pl
from jax.experimental.pallas import tpu as pltpu
from jax.sharding import PartitionSpec as P

MESH = pl.DeviceIdType.MESH
EPS = 1e-06
D = 3072
HD = 128
LOW = -1e30
NC = 4
CW = D // NC


def pick(cond, a, b):
    return jnp.where(cond, a, b)


def kernel(
    tokens_in, shift_in, scale_in, gate_in, wq_ref, wk_ref, wv_ref, qg_in, kg_in, wo_ref, lists_in, counts_in,
    out_ref,
    tokens_ref, shift_ref, scale_ref, gate_ref, qg_ref, kg_ref,
    w, wo, tok, lst, cnt, tabv, tabs, stq, stkv, qbuf, kv, kvp, m, l, o, attb, atts, part, rfwd, ra, rb, rz, zsend,
    isem, wsem, lsem, tsend, trecv, ssend, srecv, ksend, krecv, asend, arecv, rsend, rrecv,
):
    s = lax.axis_index("seq")
    u = lax.axis_index("uly")
    zl, x, c = s // 8, (s // 2) % 4, s % 2
    i, p = zl % 2, zl // 2
    y, zh = u // 2, u % 2
    d = 1 - 2 * c

    def xdev(e):
        return (zl * 8 + ((x + e + 8) % 4) * 2 + c, u)

    def yy(e):
        return (y + e + 8) % 4

    def ydev(e):
        return (s, yy(e) * 2 + zh)

    core_dev = (s + 1 - 2 * c, u)
    pair_dev = (s + 8 * (1 - 2 * i), u)
    far_dev = (s + 16 * (1 - 2 * p), u)
    anti_dev = (s, y * 2 + 1 - zh)

    def rcopy(src, dst, ss, rs, dev):
        return pltpu.make_async_remote_copy(
            src_ref=src, dst_ref=dst, send_sem=ss, recv_sem=rs, device_id=dev, device_id_type=MESH
        )

    icopies = [
        pltpu.make_async_copy(src, dst, isem.at[n])
        for n, (src, dst) in enumerate(
            (
                (tokens_in, tokens_ref),
                (scale_in, scale_ref),
                (shift_in, shift_ref),
                (lists_in, lst.at[i]),
                (counts_in, cnt.at[i]),
                (qg_in, qg_ref),
                (kg_in, kg_ref),
                (gate_in, gate_ref),
            )
        )
    ]
    wcopies = [pltpu.make_async_copy(r, w.at[n], wsem.at[n]) for n, r in enumerate((wq_ref, wk_ref, wv_ref))]
    wcopies.append(pltpu.make_async_copy(wo_ref, wo, wsem.at[3]))
    for cp in icopies + wcopies:
        cp.start()

    barrier = pltpu.get_barrier_semaphore()
    for dev in (core_dev, pair_dev, far_dev, anti_dev, xdev(1), xdev(-1), ydev(1), ydev(-1)):
        pl.semaphore_signal(barrier, inc=1, device_id=dev, device_id_type=MESH)

    for cp in icopies:
        cp.wait()
    vals = tokens_ref[...].astype(jnp.float32)
    center = jnp.mean(vals, axis=-1, keepdims=True)
    vals = vals - center
    spread = jnp.mean(vals * vals, axis=-1, keepdims=True)
    vals = vals * lax.rsqrt(spread + EPS)
    tok[0, y] = (vals * (1.0 + scale_ref[...]) + shift_ref[...]).astype(jnp.bfloat16)

    pl.semaphore_wait(barrier, 8)

    def half_rows(n):
        return pl.ds(32 * n, 32)

    def t_anti(n):
        return rcopy(tok.at[0, y, half_rows(n)], tok.at[1, y, half_rows(n)], tsend.at[n], trecv.at[n], anti_dev)

    def t_own(e):
        k = 2 if e == 1 else 3
        return rcopy(tok.at[0, y], tok.at[0, y], tsend.at[k], trecv.at[k], ydev(d * e))

    def t_own_in(e):
        k = 2 if e == 1 else 3
        sl = yy(-d * e)
        return rcopy(tok.at[0, sl], tok.at[0, sl], tsend.at[k], trecv.at[k], ydev(d * e))

    def t_fwd():
        sl = yy(-d)
        return rcopy(tok.at[0, sl], tok.at[0, sl], tsend.at[4], trecv.at[4], ydev(d))

    def t_fwd_in():
        sl = yy(2)
        return rcopy(tok.at[0, sl], tok.at[0, sl], tsend.at[4], trecv.at[4], ydev(d))

    def t_other(n, e, sl):
        k = 5 + 2 * n + (0 if e == 1 else 1)
        return rcopy(tok.at[1, sl, half_rows(n)], tok.at[1, sl, half_rows(n)], tsend.at[k], trecv.at[k], ydev(d * e))

    def t_other_fwd(n, sl):
        k = 9 + n
        return rcopy(tok.at[1, sl, half_rows(n)], tok.at[1, sl, half_rows(n)], tsend.at[k], trecv.at[k], ydev(d))

    def l_copy(row):
        return rcopy(lst.at[row], lst.at[row], lsem.at[0], lsem.at[1], pair_dev)

    def c_copy(row):
        return rcopy(cnt.at[row], cnt.at[row], lsem.at[2], lsem.at[3], pair_dev)

    l_copy(i).start()
    c_copy(i).start()
    t_anti(0).start()
    t_own(1).start()
    t_own(-1).start()
    t_anti(1).start()

    m[...] = jnp.full(m.shape, LOW, jnp.float32)
    l[...] = jnp.zeros(l.shape, jnp.float32)
    o[...] = jnp.zeros(o.shape, jnp.float32)
    l_copy(1 - i).wait_recv()
    c_copy(1 - i).wait_recv()
    listed = jnp.concatenate([lst[0], lst[1]], axis=0)
    lane = lax.broadcasted_iota(jnp.int32, (8, 128), 1)
    row = lax.broadcasted_iota(jnp.int32, (8, 128), 0)
    counts = jnp.zeros((8, 128), jnp.int32)
    for e in range(8):
        counts = jnp.where(row == e, cnt[e // 4][:, e % 4 : e % 4 + 1], counts)
    member = jnp.zeros((8, 128), jnp.int32)
    for e in range(50):
        member = jnp.where((listed[:, e : e + 1] == lane) & (e < counts), 1, member)
    union = jnp.where(
        row < 4,
        jnp.max(member[0:4], axis=0, keepdims=True),
        jnp.max(member[4:8], axis=0, keepdims=True),
    )

    def ahead(a, n):
        return a if n == 0 else pltpu.roll(a, 128 - n, 1)

    us = [ahead(union, n) > 0 for n in range(4)]
    ms = [ahead(member, n) for n in range(4)]
    f0 = 2 * p * 8 + x * 2 + c
    near = jnp.abs((lane >> 2) - jnp.where(row < 4, f0, f0 + 8)) <= 1
    idx0 = jnp.where(us[0], 0, jnp.where(us[1], 1, jnp.where(us[2], 2, 3)))
    idx1 = jnp.where(us[3], 3, jnp.where(us[2], 2, jnp.where(us[1], 1, 0)))
    idx1 = jnp.where(idx1 == idx0, (idx0 + 1) & 3, idx1)
    idx0 = jnp.where(near, 0, idx0)
    idx1 = jnp.where(near, 1, idx1)

    def at(idx):
        return jnp.where(idx == 0, ms[0], jnp.where(idx == 1, ms[1], jnp.where(idx == 2, ms[2], ms[3])))

    tabv[0] = idx0
    tabv[1] = idx1
    tabv[2] = at(idx0)
    tabv[3] = at(idx1)
    tcopy = pltpu.make_async_copy(tabv, tabs, wsem.at[4])
    tcopy.start()
    tcopy.wait()
    l_copy(i).wait_send()
    c_copy(i).wait_send()

    for cp in wcopies[:3]:
        cp.wait()

    slot_own = p * 8 + x * 2 + c

    def head_norm(piece, gain):
        power = jnp.mean(piece * piece, axis=-1, keepdims=True)
        return piece * lax.rsqrt(power + EPS) * gain[...]

    def project(h):
        a = tok[h].reshape(256, D)
        for n in (1, 2):
            acc = jnp.dot(a, w[n], preferred_element_type=jnp.float32)
            for hd in range(2):
                piece = acc[:, hd * HD : (hd + 1) * HD]
                if n == 1:
                    piece = head_norm(piece, kg_ref)
                stkv[h, hd, n - 1] = piece.astype(jnp.bfloat16)
        s_kv(h, i).start()
        kv[slot_own, h, i] = stkv[h, i]
        acc = jnp.dot(a, w[0], preferred_element_type=jnp.float32)
        for hd in range(2):
            piece = head_norm(acc[:, hd * HD : (hd + 1) * HD], qg_ref)
            stq[h, hd] = jnp.transpose(piece).astype(jnp.bfloat16)
        s_q(h, i).start()
        qbuf[i, h] = stq[h, i]

    def s_kv(h, who):
        return rcopy(stkv.at[h, 1 - i], kv.at[slot_own, h, who], ssend.at[h, 0], srecv.at[h, 0], pair_dev)

    def s_q(h, who):
        return rcopy(stq.at[h, 1 - i], qbuf.at[who, h], ssend.at[h, 1], srecv.at[h, 1], pair_dev)

    def k_copy(h, ff, slot, e, dev):
        return rcopy(kv.at[slot, h, ff], kv.at[slot, h, ff], ksend.at[h, ff, e], krecv.at[h, ff, slot], dev)

    def swap_in(h):
        def send(ff):
            k_copy(h, ff, slot_own, 0, far_dev).start()
            k_copy(h, ff, slot_own, 1, xdev(1)).start()
            k_copy(h, ff, slot_own, 2, xdev(-1)).start()
            k_copy(h, ff, slot_own, 3, core_dev).start()

        send(i)
        s_kv(h, 1 - i).wait_recv()
        send(1 - i)
        s_q(h, 1 - i).wait_recv()

    t_own_in(1).wait_recv()
    t_fwd().start()
    t_anti(0).wait_recv()
    t_other(0, 1, y).start()
    t_other(0, -1, y).start()
    t_own_in(-1).wait_recv()
    t_fwd_in().wait_recv()
    project(0)
    t_anti(1).wait_recv()
    t_other(1, 1, y).start()
    t_other(1, -1, y).start()
    t_other(0, 1, yy(-d)).wait_recv()
    t_other_fwd(0, yy(-d)).start()
    swap_in(0)

    factor = (HD ** -0.5) * math.log2(math.e)
    lane1 = lax.broadcasted_iota(jnp.int32, (1, 128), 1)

    def attend(fi, h, parts):
        q = qbuf[fi, h]
        old = m[fi, h, 0:1]
        new = old
        tiles = []
        for keys, _, bias in parts:
            scores = jnp.dot(keys, q, preferred_element_type=jnp.float32) * factor
            if bias is not None:
                scores = (scores.reshape(4, 64, 256) + bias).reshape(256, 256)
            tiles.append(scores)
            new = jnp.maximum(new, jnp.max(scores, axis=0, keepdims=True))
        decay = jnp.exp2(old - new)
        total = l[fi, h, 0:1] * decay
        summed = o[fi, h] * decay
        for scores, (_, values, _) in zip(tiles, parts):
            weights = jnp.exp2(scores - new)
            total = total + jnp.sum(weights, axis=0, keepdims=True)
            summed = summed + jnp.dot(values, weights.astype(jnp.bfloat16), preferred_element_type=jnp.float32)
        m[fi, h, 0:1] = new
        l[fi, h, 0:1] = total
        o[fi, h] = summed

    def near_pass(n, carry):
        fi, df = n // 3, n % 3 - 1
        f = (2 * p + fi) * 8 + x * 2 + c + df

        @pl.when(jnp.logical_and(f >= 0, f <= 31))
        def _():
            fz = f // 8
            slot = (fz // 2) * 8 + f % 8
            keys = jnp.concatenate([kv[slot, h, fz % 2, 0, 128:256] for h in range(2)], axis=0)
            values = jnp.transpose(
                jnp.concatenate([kv[slot, h, fz % 2, 1, 128:256] for h in range(2)], axis=0)
            )
            for h in range(2):
                attend(fi, h, [(keys, values, None)])

        return carry

    def chosen(fi, base):
        rows, bias = [], []
        for ff in range(2):
            at4 = (base + 8 * ff) * 4
            rows.append([tabs[t, fi * 4, at4] for t in range(2)])
            for t in range(2):
                b = [jnp.where(tabs[2 + t, fi * 4 + e, at4] > 0, 0.0, LOW) for e in range(4)]
                across = [jnp.where(lane1 < 64, b[2 * e], b[2 * e + 1]) for e in range(2)]
                bias.append(jnp.concatenate(across, axis=1).reshape(1, 1, 256))
        bias = jnp.concatenate(bias, axis=0)

        def group(oc):
            keys, values = (
                jnp.concatenate([kvp[oc, ff, t, rows[ff][e]] for ff in range(2) for e in range(2)], axis=0)
                for t in range(2)
            )
            return keys, jnp.transpose(values), bias

        return group

    def slot_of(j, oc):
        dp = pick(j == 3, 1, pick(j >= 5, 1, 0))
        dxs = pick(j % 4 == 1, -1, pick(j == 2, 1, pick(j == 6, 1, pick(j == 4, 2, pick(j == 7, 2, 0)))))
        dd = d * (1 - 2 * oc)
        return ((p + dp) % 2) * 8 + ((x + dd * dxs + 8) % 4) * 2 + (c + oc) % 2

    def arrive(h, j):
        slot = slot_of(j, 0)
        for ff in range(2):

            @pl.when(j > 0)
            def _():
                k_copy(h, ff, slot, 0, core_dev).wait_recv()

            @pl.when(j % 4 == 1)
            def _():
                k_copy(h, ff, slot, 11 + j // 4, xdev(d)).start()

            @pl.when(j == 3)
            def _():
                k_copy(h, ff, slot, 13, xdev(1)).start()
                k_copy(h, ff, slot, 14, xdev(-1)).start()

            @pl.when(j > 0)
            def _():
                k_copy(h, ff, slot, 3 + j, core_dev).start()

    def arrive_other(h, j):
        for ff in range(2):
            k_copy(h, ff, slot_of(j, 1), 0, core_dev).wait_recv()

    def consume(h, j, halves):
        slots = [slot_of(j, oc) for oc in range(2)]
        for oc in range(2):
            kvp[oc] = kv[slots[oc], h].reshape(2, 2, 4, 64, HD)
        for fi in range(2):
            parts = [chosen(fi, (slot // 8) * 16 + slot % 8)(oc) for oc, slot in enumerate(slots)]
            for qh in halves:
                attend(fi, qh, parts)

    def phase0(j, carry):
        @pl.when(j == 1)
        def _():
            t_other(1, 1, yy(-d)).wait_recv()
            t_other_fwd(1, yy(-d)).start()

        @pl.when(j == 2)
        def _():
            for e in range(2):
                t_other(e, -1, yy(d)).wait_recv()
                t_other_fwd(e, yy(2)).wait_recv()
            project(1)

        @pl.when(j == 4)
        def _():
            swap_in(1)

        @pl.when(j == 7)
        def _():
            arrive(1, 1)

        arrive(0, j)

        @pl.when(j >= 4)
        def _():
            consume(0, j - 4, (1,))

        arrive_other(0, j)
        consume(0, j, (0,))
        return carry

    def phase1(j, carry):
        @pl.when(jnp.logical_and(j > 4, j < 7))
        def _():
            arrive(1, j - 3)

        consume(0, j, (1,))
        return carry

    def phase2(j, carry):
        @pl.when(jnp.logical_and(j >= 2, j <= 5))
        def _():
            arrive(1, j + 2)

        @pl.when(j == 7)
        def _():
            lax.fori_loop(0, 6, near_pass, 0)

        arrive_other(1, j)
        consume(1, j, (0, 1))
        return carry

    lax.fori_loop(0, 8, phase0, 0)
    lax.fori_loop(4, 8, phase1, 0)
    lax.fori_loop(0, 8, phase2, 0)

    def result(fi, h):
        return jnp.transpose(o[fi, h] / l[fi, h, 0:1]).astype(jnp.bfloat16)

    def a_copy(h, head):
        return rcopy(atts.at[h], attb.at[head, h], asend.at[h], arecv.at[h], pair_dev)

    for h in (1, 0):
        atts[h] = result(1 - i, h)
        a_copy(h, i).start()
    for h in (1, 0):
        attb[i, h] = result(i, h)
    wcopies[3].wait()

    def r_out(q, dest):
        return rcopy(part.at[q, dest], rfwd.at[q], rsend.at[q, 0], rrecv.at[q, 0], ydev(d))

    def r_a(q):
        return rcopy(part.at[q, yy(d)], ra.at[q], rsend.at[q, 1], rrecv.at[q, 1], ydev(d))

    def r_b(q):
        return rcopy(part.at[q, yy(-d)], rb.at[q], rsend.at[q, 2], rrecv.at[q, 2], ydev(-d))

    def r_z(cc):
        return rcopy(zsend.at[cc], rz.at[cc], rsend.at[NC + cc, 3], rrecv.at[NC + cc, 3], anti_dev)

    def out_project(h, cc, rows):
        q = NC * h + cc
        res = jnp.dot(rows, wo[:, cc * CW : (cc + 1) * CW], preferred_element_type=jnp.float32)
        part[q] = res.astype(jnp.bfloat16).reshape(4, 64, CW)

    def out_sends(first):
        for q in (first, first + 1):
            r_out(q, yy(2)).start()

    def chain(first):
        for q in (first, first + 1):
            r_out(q, yy(2)).wait_recv()
            part[q, yy(d)] = (part[q, yy(d)].astype(jnp.float32) + rfwd[q].astype(jnp.float32)).astype(jnp.bfloat16)
            r_a(q).start()
            r_b(q).start()

    def gathered(q):
        r_a(q).wait_recv()
        r_b(q).wait_recv()
        return part[q, y].astype(jnp.float32) + ra[q].astype(jnp.float32) + rb[q].astype(jnp.float32)

    def to_anti(first):
        for cc in (first, first + 1):
            zsend[cc] = gathered(NC + cc).astype(jnp.bfloat16)
            r_z(cc).start()

    for h in (1, 0):
        a_copy(h, 1 - i).wait_recv()
        rows = jnp.concatenate([attb[0, h], attb[1, h]], axis=1)
        for cc in range(NC):
            out_project(h, cc, rows)
            if h == 1 and cc == 1:
                out_sends(NC)
    out_sends(NC + 2)
    chain(NC)
    out_sends(0)
    chain(NC + 2)
    to_anti(0)
    out_sends(2)
    chain(0)
    to_anti(2)
    chain(2)
    for cc in range(NC):
        total = gathered(cc)
        r_z(cc).wait_recv()
        cols = slice(cc * CW, (cc + 1) * CW)
        out_ref[:, cols] = ((total + rz[cc].astype(jnp.float32)) * gate_ref[:, cols]).astype(jnp.bfloat16)

    for n in range(2):
        t_anti(n).wait_send()
        t_other(n, 1, y).wait_send()
        t_other(n, -1, y).wait_send()
        t_other_fwd(n, yy(-d)).wait_send()
    t_own(1).wait_send()
    t_own(-1).wait_send()
    t_fwd().wait_send()
    for h in range(2):
        s_kv(h, i).wait_send()
        s_q(h, i).wait_send()
        a_copy(h, i).wait_send()
        for ff in range(2):
            for e in range(15):
                k_copy(h, ff, slot_own, e, core_dev).wait_send()
    for q in range(2 * NC):
        r_out(q, yy(2)).wait_send()
        r_a(q).wait_send()
        r_b(q).wait_send()
    for cc in range(NC):
        r_z(cc).wait_send()


def body(tokens, mod_shift, mod_scale, mod_gate, w_query, w_key, w_value, q_gain, k_gain, w_out, kv_blocks, kv_count):
    vmem = pl.BlockSpec(memory_space=pltpu.VMEM)
    hbm = pl.BlockSpec(memory_space=pltpu.HBM)
    bf16, f32, i32 = jnp.bfloat16, jnp.float32, jnp.int32
    dma = pltpu.SemaphoreType.DMA
    return pl.pallas_call(
        kernel,
        out_shape=jax.ShapeDtypeStruct((64, D), bf16),
        in_specs=[hbm] * 12,
        out_specs=vmem,
        scratch_shapes=[
            pltpu.VMEM((64, D), bf16),
            pltpu.VMEM((1, D), f32),
            pltpu.VMEM((1, D), f32),
            pltpu.VMEM((1, D), f32),
            pltpu.VMEM((1, HD), f32),
            pltpu.VMEM((1, HD), f32),
            pltpu.VMEM((3, D, 256), bf16),
            pltpu.VMEM((256, D), bf16),
            pltpu.VMEM((2, 4, 64, D), bf16),
            pltpu.VMEM((2, 4, 50), i32),
            pltpu.VMEM((2, 1, 4), i32),
            pltpu.VMEM((4, 8, 128), i32),
            pltpu.SMEM((4, 8, 128), i32),
            pltpu.VMEM((2, 2, HD, 256), bf16),
            pltpu.VMEM((2, 2, 2, 256, HD), bf16),
            pltpu.VMEM((2, 2, HD, 256), bf16),
            pltpu.VMEM((16, 2, 2, 2, 256, HD), bf16),
            pltpu.VMEM((2, 2, 2, 4, 64, HD), bf16),
            pltpu.VMEM((2, 2, 8, 256), f32),
            pltpu.VMEM((2, 2, 8, 256), f32),
            pltpu.VMEM((2, 2, HD, 256), f32),
            pltpu.VMEM((2, 2, 256, HD), bf16),
            pltpu.VMEM((2, 256, HD), bf16),
            pltpu.VMEM((2 * NC, 4, 64, CW), bf16),
            pltpu.VMEM((2 * NC, 64, CW), bf16),
            pltpu.VMEM((2 * NC, 64, CW), bf16),
            pltpu.VMEM((2 * NC, 64, CW), bf16),
            pltpu.VMEM((NC, 64, CW), bf16),
            pltpu.VMEM((NC, 64, CW), bf16),
            dma((8,)),
            dma((5,)),
            dma((4,)),
            dma((11,)),
            dma((11,)),
            dma((2, 2)),
            dma((2, 2)),
            dma((2, 2, 15)),
            dma((2, 2, 16)),
            dma((2,)),
            dma((2,)),
            dma((2 * NC, 4)),
            dma((2 * NC, 4)),
        ],
        compiler_params=pltpu.CompilerParams(
            collective_id=0, has_side_effects=True, vmem_limit_bytes=56 * 2**20
        ),
        name="radial_block",
    )(
        tokens,
        mod_shift.reshape(1, D),
        mod_scale.reshape(1, D),
        mod_gate.reshape(1, D),
        w_query,
        w_key,
        w_value,
        q_gain.reshape(1, HD),
        k_gain.reshape(1, HD),
        w_out,
        kv_blocks,
        kv_count.reshape(1, 4),
    )


def solution(mesh):
    placed = (
        P(("seq", "uly"), None),
        P(),
        P(),
        P(),
        P(None, "uly"),
        P(None, "uly"),
        P(None, "uly"),
        P(),
        P(),
        P("uly", None),
        P("seq", None),
        P("seq"),
    )
    return jax.shard_map(
        body, mesh=mesh, in_specs=placed, out_specs=P(("seq", "uly"), None), check_vma=False
    )
```

time: 152 us -> 124 us (0.82)
  Pallas kernels: 141 us -> 120 us
  local copies, waits for them, and re-layouts: 10.1 us -> 1.77 us
    pallas_call x1, Pallas kernels: 141 us -> 120 us  [body(): pl.pallas_call(kernel, out_shape=jax.ShapeDtypeStruct((64, D), bf16), in_...]
    unnamed x19 -> x1, local copies, waits for them, and re-layouts: 9.39 us -> 1.77 us
where the time goes in v2:
time: 124 us; the launch traced here: 122 us
  Pallas kernels  120 us (97%)
  local copies, waits for them, and re-layouts  1.77 us (1%)
    pallas_call x1, Pallas kernels, body(): pl.pallas_call(kernel, out_shape=jax.ShapeDtypeStruct((64, D), bf16), in_...  120 us

profile of v2, /device:TPU:8, one launch (start us, length us, event | category | flops | bytes accessed | tf_op | source)
XLA Modules:
  0.0 122.3 jit_solution(1158119397552418916)
XLA Ops:
  0.0 120.5 %radial_block.1 = bf16[64,3072]{1,0:T(8,128)(2,1)} custom-call(bf16[64,3072]{1,0:T(8,128)(2,1)} %tokens_in.1, f32[1,3072]{1,0:T(1,128)} %bitcast.6, f32[1,3072]{1,0:T(1,128)} %bitcast.7, f32[1,3072]{1,0:T(1,128)} %bitcast.8, bf16[3072,256]{1,0:T(8,128)(2,1)} %wq_ref.1, bf16[3072,256]{1,0:T(8,128)(2,1)} %wk_ref.1, bf16[3072,256]{1,0:T(8,128)(2,1)} %wv_ref.1, ...), custom_call_target="tpu_custom_call" | custom-call | tf_op jit(solution)/shard_map/radial_block/pallas_call | solution.py:504
  120.5 1.8 %copy.14 = bf16[64,3072]{1,0:T(8,128)(2,1)} copy(bf16[64,3072]{1,0:T(8,128)(2,1)} %radial_block.1) | data formatting | bytes 786432

commit v3 on v2

--- a/solution.py
+++ b/solution.py
@@ -253,7 +253,7 @@
         for keys, _, bias in parts:
             scores = jnp.dot(keys, q, preferred_element_type=jnp.float32) * factor
             if bias is not None:
-                scores = (scores.reshape(4, 64, 256) + bias).reshape(256, 256)
+                scores = (scores.reshape(bias.shape[0], -1, 256) + bias).reshape(scores.shape)
             tiles.append(scores)
             new = jnp.maximum(new, jnp.max(scores, axis=0, keepdims=True))
         decay = jnp.exp2(old - new)
@@ -267,22 +267,22 @@
         l[fi, h, 0:1] = total
         o[fi, h] = summed
 
-    def near_pass(n, carry):
-        fi, df = n // 3, n % 3 - 1
-        f = (2 * p + fi) * 8 + x * 2 + c + df
-
-        @pl.when(jnp.logical_and(f >= 0, f <= 31))
-        def _():
+    def near(half, fi):
+        keys, values, bias = [], [], []
+        for df in (-1, 0, 1):
+            f = (2 * p + fi) * 8 + x * 2 + c + df
+            inside = jnp.logical_and(f >= 0, f <= 31)
+            f = (f + 32) % 32
             fz = f // 8
             slot = (fz // 2) * 8 + f % 8
-            keys = jnp.concatenate([kv[slot, h, fz % 2, 0, 128:256] for h in range(2)], axis=0)
-            values = jnp.transpose(
-                jnp.concatenate([kv[slot, h, fz % 2, 1, 128:256] for h in range(2)], axis=0)
-            )
-            for h in range(2):
-                attend(fi, h, [(keys, values, None)])
-
-        return carry
+            keys.append(kv[slot, half, fz % 2, 0, 128:256])
+            values.append(kv[slot, half, fz % 2, 1, 128:256])
+            bias.append(jnp.broadcast_to(jnp.where(inside, 0.0, LOW), (1, 128, 256)))
+        keys = jnp.concatenate(keys, axis=0)
+        values = jnp.transpose(jnp.concatenate(values, axis=0))
+        bias = jnp.concatenate(bias, axis=0)
+        for h in range(2):
+            attend(fi, h, [(keys, values, bias)])
 
     def chosen(fi, base):
         rows, bias = [], []
@@ -345,7 +345,7 @@
                 attend(fi, qh, parts)
 
     def phase0(j, carry):
-        @pl.when(j == 1)
+        @pl.when(j == 0)
         def _():
             t_other(1, 1, yy(-d)).wait_recv()
             t_other_fwd(1, yy(-d)).start()
@@ -381,19 +381,31 @@
             arrive(1, j - 3)
 
         consume(0, j, (1,))
+
+        @pl.when(j == 7)
+        def _():
+            near(0, 0)
+            near(0, 1)
+
         return carry
 
     def phase2(j, carry):
-        @pl.when(jnp.logical_and(j >= 2, j <= 5))
+        @pl.when(jnp.logical_or(j == 2, j == 3))
         def _():
             arrive(1, j + 2)
 
         @pl.when(j == 7)
         def _():
-            lax.fori_loop(0, 6, near_pass, 0)
+            near(1, 0)
+            near(1, 1)
 
         arrive_other(1, j)
         consume(1, j, (0, 1))
+
+        @pl.when(jnp.logical_or(j == 4, j == 5))
+        def _():
+            arrive(1, j + 2)
+
         return carry
 
     lax.fori_loop(0, 8, phase0, 0)

time: 124 us -> 121 us (0.976)
  Pallas kernels: 120 us -> 118 us
    pallas_call x1, Pallas kernels: 120 us -> 118 us  [body(): pl.pallas_call(kernel, out_shape=jax.ShapeDtypeStruct((64, D), bf16), in_...]
where the time goes in v3:
time: 121 us; the launch traced here: 119 us
  Pallas kernels  118 us (98%)
  local copies, waits for them, and re-layouts  1.77 us (1%)
    pallas_call x1, Pallas kernels, body(): pl.pallas_call(kernel, out_shape=jax.ShapeDtypeStruct((64, D), bf16), in_...  118 us

profile of v3, /device:TPU:8, one launch (start us, length us, event | category | flops | bytes accessed | tf_op | source)
XLA Modules:
  0.0 119.5 jit_solution(18232021561152727244)
XLA Ops:
  0.0 117.7 %radial_block.1 = bf16[64,3072]{1,0:T(8,128)(2,1)} custom-call(bf16[64,3072]{1,0:T(8,128)(2,1)} %tokens_in.1, f32[1,3072]{1,0:T(1,128)} %bitcast.6, f32[1,3072]{1,0:T(1,128)} %bitcast.7, f32[1,3072]{1,0:T(1,128)} %bitcast.8, bf16[3072,256]{1,0:T(8,128)(2,1)} %wq_ref.1, bf16[3072,256]{1,0:T(8,128)(2,1)} %wk_ref.1, bf16[3072,256]{1,0:T(8,128)(2,1)} %wv_ref.1, ...), custom_call_target="tpu_custom_call" | custom-call | tf_op jit(solution)/shard_map/radial_block/pallas_call | solution.py:516
  117.7 1.8 %copy.14 = bf16[64,3072]{1,0:T(8,128)(2,1)} copy(bf16[64,3072]{1,0:T(8,128)(2,1)} %radial_block.1) | data formatting | bytes 786432
